TPU v7x, 32 devices: a whole 2x2x4 slice. The times are simulated.
32 devices in a mesh: dp: 8 (over y, x, core), seq: 4 (over z).
Axes of the slice: x: 2, y: 2, z: 4, core: 2. Of those that a mesh axis runs over, the one named last changes fastest.
Arguments:
- tokens: bfloat16 [24, 1024, 768], P('dp', 'seq'), may hold values from -6 to 6
- cond: bfloat16 [24, 128], P('dp'), may hold values from -6 to 6
- lengths: int32 [24], P('dp'), may hold values from 128 to 1024, as said below
- gain_one: float32 [768], replicated, may hold values from 0.1 to 1.9
- gain_two: float32 [768], replicated, may hold values from 0.1 to 1.9
- w_ada: bfloat16 [128, 4608], replicated, may hold values from -0.5 to 0.5
- b_ada: float32 [4608], replicated, may hold values from -3 to 3
- w_qkv: bfloat16 [768, 2304], replicated, may hold values from -0.21875 to 0.21875
- w_out: bfloat16 [768, 768], replicated, may hold values from -0.3125 to 0.3125
- w_up: bfloat16 [768, 3072], replicated, may hold values from -0.21875 to 0.21875
- b_up: float32 [3072], replicated, may hold values from -3 to 3
- w_down: bfloat16 [3072, 768], replicated, may hold values from -0.109375 to 0.109375
- b_down: float32 [768], replicated, may hold values from -3 to 3
- cotangent: bfloat16 [24, 1024, 768], P('dp', 'seq'), may hold values from -8 to 8
Outputs:
- output: bfloat16 [24, 1024, 768], P('dp', 'seq')
- grad_tokens: float32 [24, 1024, 768], P('dp', 'seq')
- grad_cond: float32 [24, 128], P('dp')
- grad_gain_one: float32 [768], P(('dp', 'seq'))
- grad_gain_two: float32 [768], P(('dp', 'seq'))
- grad_w_ada: float32 [128, 4608], P(None, ('dp', 'seq'))
- grad_b_ada: float32 [4608], P(('dp', 'seq'))
- grad_w_qkv: float32 [768, 2304], P(('dp', 'seq'))
- grad_w_out: float32 [768, 768], P(('dp', 'seq'))
- grad_w_up: float32 [768, 3072], P(('dp', 'seq'))
- grad_b_up: float32 [3072], P(('dp', 'seq'))
- grad_w_down: float32 [3072, 768], P(('dp', 'seq'))
- grad_b_down: float32 [768], P(('dp', 'seq'))
Inputs may be any that keep to these rules, and one draw needn't show every extreme that they name: `lengths`: each length is 128, 512 or 1024, each sequence's drawn independently; some sequence of the batch has 1024 and some other has 128.
All inputs are finite; a program needn't handle non-finite values.
Results may differ from a plain program's by a relative error of at most 0.015.
The roundings to bfloat16 on the way count: a program that leaves them out, or rounds other values in their place, can miss the bound.
Values may be sent and summed in bfloat16 or wider, within the bound.
No kernel may reach another device: no remote copies, remote signals or barrier semaphores. Data moves between devices by JAX's collectives and lax.ppermute only.
A program may use at most 256 MiB of HBM per device.

v0:
```python
import jax
import jax.numpy as jnp
from jax import lax
from jax.sharding import PartitionSpec as P

HEADS = 12
HD = 64


EPS = 1e-05
NEG = -1e30
HIGH = lax.Precision.HIGHEST


def normalize(vector):
    average = jnp.mean(vector, axis=-1, keepdims=True)
    centred = vector - average
    inverse = lax.rsqrt(jnp.mean(centred * centred, axis=-1, keepdims=True) + EPS)
    return (centred * inverse, inverse)


def norm_back(grad_normed, normed, inverse):
    return inverse * (
        grad_normed
        - jnp.mean(grad_normed, axis=-1, keepdims=True)
        - normed * jnp.mean(grad_normed * normed, axis=-1, keepdims=True)
    )


def rotate(vector, cosine, sine_table):
    half_width = vector.shape[-1] // 2
    front_half = vector[..., :half_width]
    back_half = vector[..., half_width:]
    return jnp.concatenate(
        [
            front_half * cosine - back_half * sine_table,
            back_half * cosine + front_half * sine_table,
        ],
        axis=-1,
    )


def masked_scores(query_rows, key_rows, length):
    scores = jnp.einsum(
        "qhe,khe->hqk", query_rows, key_rows, preferred_element_type=jnp.float32
    ) * HD ** (-0.5)
    usable = jnp.arange(key_rows.shape[0]) < length
    return jnp.where(usable[None, None, :], scores, NEG)


def attend(queries, keys_all, values_all, lengths):

    def single(element):
        query_rows, key_rows, value_rows, length = element
        scores = masked_scores(query_rows, key_rows, length)
        row_max = jnp.max(scores, axis=-1, keepdims=True)
        raised = jnp.exp(scores - row_max)
        row_sum = jnp.sum(raised, axis=-1, keepdims=True)
        weights_rounded = (raised / row_sum).astype(jnp.bfloat16)
        mixture = jnp.einsum(
            "hqk,khe->qhe", weights_rounded, value_rows, preferred_element_type=jnp.float32
        )
        return (mixture.astype(jnp.bfloat16), row_max[..., 0] + jnp.log(row_sum[..., 0]))

    return lax.map(single, (queries, keys_all, values_all, lengths))


def attend_back(queries, keys_all, values_all, lengths, grad_mixture, log_totals):

    def single(element):
        query_rows, key_rows, value_rows, length, grad_rows, log_rows = element
        scores = masked_scores(query_rows, key_rows, length)
        exact = jnp.exp(scores - log_rows[..., None])
        grad_values = jnp.einsum(
            "hqk,qhe->khe",
            exact.astype(jnp.bfloat16),
            grad_rows,
            preferred_element_type=jnp.float32,
        )
        grad_exact = jnp.einsum(
            "qhe,khe->hqk", grad_rows, value_rows, preferred_element_type=jnp.float32
        )
        inner_sum = jnp.sum(exact * grad_exact, axis=-1, keepdims=True)
        grad_scores = (exact * (grad_exact - inner_sum)).astype(jnp.bfloat16)
        grad_queries = jnp.einsum(
            "hqk,khe->qhe", grad_scores, key_rows, preferred_element_type=jnp.float32
        ) * HD ** (-0.5)
        grad_keys = jnp.einsum(
            "hqk,qhe->khe", grad_scores, query_rows, preferred_element_type=jnp.float32
        ) * HD ** (-0.5)
        return (grad_queries, grad_keys, grad_values)

    return lax.map(single, (queries, keys_all, values_all, lengths, grad_mixture, log_totals))


def body(
    tokens,
    cond,
    lengths,
    gain_one,
    gain_two,
    w_ada,
    b_ada,
    w_qkv,
    w_out,
    w_up,
    b_up,
    w_down,
    b_down,
    cotangent,
):
    seq_count, piece_len, model_width = tokens.shape
    row_count = seq_count * piece_len
    modulation = jnp.dot(cond, w_ada, preferred_element_type=jnp.float32) + b_ada
    shift_one, scale_one, gate_one, shift_two, scale_two, gate_two = [
        modulation[:, None, block_index * model_width : (block_index + 1) * model_width]
        for block_index in range(6)
    ]
    piece_start = lax.axis_index("seq") * piece_len
    positions = (piece_start + jnp.arange(piece_len)).astype(jnp.float32)
    inverse_freq = jnp.power(10000.0, -jnp.arange(HD // 2).astype(jnp.float32) * 2.0 / HD)
    angles = positions[:, None] * inverse_freq[None, :]
    cosine = jnp.cos(angles)[:, None, :]
    sine_table = jnp.sin(angles)[:, None, :]

    def prepare(source):
        source_f = source.astype(jnp.float32)
        normed_one, inverse_one = normalize(source_f)
        scaled_one = normed_one * gain_one
        act_one = (
            (scaled_one * (1.0 + scale_one) + shift_one)
            .astype(jnp.bfloat16)
            .reshape(row_count, model_width)
        )
        projected = jnp.dot(act_one, w_qkv, preferred_element_type=jnp.float32).reshape(
            seq_count, piece_len, 3, HEADS, HD
        )
        queries = rotate(projected[:, :, 0], cosine, sine_table).astype(jnp.bfloat16)
        keys_local = rotate(projected[:, :, 1], cosine, sine_table).astype(jnp.bfloat16)
        values_local = projected[:, :, 2].astype(jnp.bfloat16)
        return (
            source_f,
            normed_one,
            inverse_one,
            scaled_one,
            act_one,
            queries,
            keys_local,
            values_local,
        )

    def finish(source_f, mixture):
        branch_one = jnp.dot(mixture, w_out, preferred_element_type=jnp.float32).reshape(
            seq_count, piece_len, model_width
        )
        residual = source_f + gate_one * branch_one
        normed_two, inverse_two = normalize(residual)
        scaled_two = normed_two * gain_two
        act_two = (
            (scaled_two * (1.0 + scale_two) + shift_two)
            .astype(jnp.bfloat16)
            .reshape(row_count, model_width)
        )
        pre_gelu = jnp.dot(act_two, w_up, preferred_element_type=jnp.float32) + b_up
        activated = jax.nn.gelu(pre_gelu, approximate=True).astype(jnp.bfloat16)
        branch_two = (
            jnp.dot(activated, w_down, preferred_element_type=jnp.float32) + b_down
        ).reshape(seq_count, piece_len, model_width)
        result = residual + gate_two * branch_two
        return (
            branch_one,
            residual,
            normed_two,
            inverse_two,
            scaled_two,
            act_two,
            pre_gelu,
            activated,
            branch_two,
            result,
        )

    early_part = prepare(tokens)
    keys_all, values_all = (
        lax.all_gather(early_part[6], "seq", axis=1, tiled=True),
        lax.all_gather(early_part[7], "seq", axis=1, tiled=True),
    )
    mixture, log_totals = attend(early_part[5], keys_all, values_all, lengths)
    mixture_rows = mixture.reshape(row_count, model_width)
    later_part = finish(early_part[0], mixture_rows)
    output = later_part[9].astype(jnp.bfloat16)
    reloaded = lax.optimization_barrier(tokens)
    early_part = prepare(reloaded)
    keys_all, values_all = (
        lax.all_gather(early_part[6], "seq", axis=1, tiled=True),
        lax.all_gather(early_part[7], "seq", axis=1, tiled=True),
    )
    mixture, log_totals = attend(early_part[5], keys_all, values_all, lengths)
    mixture_rows = mixture.reshape(row_count, model_width)
    later_part = finish(early_part[0], mixture_rows)
    source_f, normed_one, inverse_one, scaled_one, act_one, queries, keys_local, values_local = (
        early_part
    )
    (
        branch_one,
        residual,
        normed_two,
        inverse_two,
        scaled_two,
        act_two,
        pre_gelu,
        activated,
        branch_two,
        result,
    ) = later_part
    grad_out = cotangent.astype(jnp.float32)
    grad_gate_two = jnp.sum(grad_out * branch_two, axis=1)
    grad_branch_two = (grad_out * gate_two).astype(jnp.bfloat16).reshape(row_count, model_width)
    grad_b_down = jnp.sum(grad_branch_two, axis=0, dtype=jnp.float32)
    grad_w_down = jnp.einsum(
        "rf,rd->fd", activated, grad_branch_two, preferred_element_type=jnp.float32
    )
    grad_activated = jnp.dot(grad_branch_two, w_down.T, preferred_element_type=jnp.float32)
    _, gelu_pull = jax.vjp(lambda inner: jax.nn.gelu(inner, approximate=True), pre_gelu)
    grad_pre_gelu = gelu_pull(grad_activated)[0].astype(jnp.bfloat16)
    grad_b_up = jnp.sum(grad_pre_gelu, axis=0, dtype=jnp.float32)
    grad_w_up = jnp.einsum("rd,rf->df", act_two, grad_pre_gelu, preferred_element_type=jnp.float32)
    grad_act_two = jnp.dot(grad_pre_gelu, w_up.T, preferred_element_type=jnp.float32).reshape(
        seq_count, piece_len, model_width
    )
    grad_shift_two = jnp.sum(grad_act_two, axis=1)
    grad_scale_two = jnp.sum(grad_act_two * scaled_two, axis=1)
    grad_scaled_two = grad_act_two * (1.0 + scale_two)
    grad_gain_two = jnp.sum(grad_scaled_two * normed_two, axis=(0, 1))
    grad_residual = grad_out + norm_back(grad_scaled_two * gain_two, normed_two, inverse_two)
    grad_gate_one = jnp.sum(grad_residual * branch_one, axis=1)
    grad_branch_one = (
        (grad_residual * gate_one).astype(jnp.bfloat16).reshape(row_count, model_width)
    )
    grad_w_out = jnp.einsum(
        "rd,re->de", mixture_rows, grad_branch_one, preferred_element_type=jnp.float32
    )
    grad_mixture = (
        jnp.dot(grad_branch_one, w_out.T, preferred_element_type=jnp.float32)
        .astype(jnp.bfloat16)
        .reshape(seq_count, piece_len, HEADS, HD)
    )
    grad_queries, grad_keys_all, grad_values_all = attend_back(
        queries, keys_all, values_all, lengths, grad_mixture, log_totals
    )
    grad_keys, grad_values = (
        lax.psum_scatter(
            grad_keys_all.astype(jnp.bfloat16), "seq", scatter_dimension=1, tiled=True
        ).astype(jnp.float32),
        lax.psum_scatter(
            grad_values_all.astype(jnp.bfloat16), "seq", scatter_dimension=1, tiled=True
        ).astype(jnp.float32),
    )
    grad_projected = jnp.stack(
        [
            rotate(grad_queries, cosine, -sine_table),
            rotate(grad_keys, cosine, -sine_table),
            grad_values,
        ],
        axis=2,
    )
    grad_projected = grad_projected.astype(jnp.bfloat16).reshape(row_count, 3 * model_width)
    grad_w_qkv = jnp.einsum(
        "rd,re->de", act_one, grad_projected, preferred_element_type=jnp.float32
    )
    grad_act_one = jnp.dot(grad_projected, w_qkv.T, preferred_element_type=jnp.float32).reshape(
        seq_count, piece_len, model_width
    )
    grad_shift_one = jnp.sum(grad_act_one, axis=1)
    grad_scale_one = jnp.sum(grad_act_one * scaled_one, axis=1)
    grad_scaled_one = grad_act_one * (1.0 + scale_one)
    grad_gain_one = jnp.sum(grad_scaled_one * normed_one, axis=(0, 1))
    grad_tokens = grad_residual + norm_back(grad_scaled_one * gain_one, normed_one, inverse_one)
    grad_modulation = jnp.concatenate(
        [
            grad_shift_one,
            grad_scale_one,
            grad_gate_one,
            grad_shift_two,
            grad_scale_two,
            grad_gate_two,
        ],
        axis=-1,
    )
    grad_w_ada = jnp.dot(cond.astype(jnp.float32).T, grad_modulation, precision=HIGH)
    grad_b_ada = jnp.sum(grad_modulation, axis=0)
    cond_share = jnp.dot(grad_modulation, w_ada.astype(jnp.float32).T, precision=HIGH)
    grad_cond = lax.psum(cond_share, "seq")
    summed = (
        lax.psum_scatter(grad_gain_one, ("dp", "seq"), scatter_dimension=0, tiled=True),
        lax.psum_scatter(grad_gain_two, ("dp", "seq"), scatter_dimension=0, tiled=True),
        lax.psum_scatter(grad_w_ada, ("dp", "seq"), scatter_dimension=1, tiled=True),
        lax.psum_scatter(grad_b_ada, ("dp", "seq"), scatter_dimension=0, tiled=True),
        lax.psum_scatter(grad_w_qkv, ("dp", "seq"), scatter_dimension=0, tiled=True),
        lax.psum_scatter(grad_w_out, ("dp", "seq"), scatter_dimension=0, tiled=True),
        lax.psum_scatter(grad_w_up, ("dp", "seq"), scatter_dimension=0, tiled=True),
        lax.psum_scatter(grad_b_up, ("dp", "seq"), scatter_dimension=0, tiled=True),
        lax.psum_scatter(grad_w_down, ("dp", "seq"), scatter_dimension=0, tiled=True),
        lax.psum_scatter(grad_b_down, ("dp", "seq"), scatter_dimension=0, tiled=True),
    )
    return (
        output,
        grad_tokens,
        grad_cond,
        summed[0],
        summed[1],
        summed[2],
        summed[3],
        summed[4],
        summed[5],
        summed[6],
        summed[7],
        summed[8],
        summed[9],
    )


def solution(mesh):
    placed = (
        P("dp", "seq", None),
        P("dp", None),
        P("dp"),
        P(),
        P(),
        P(),
        P(),
        P(),
        P(),
        P(),
        P(),
        P(),
        P(),
        P("dp", "seq", None),
    )
    return jax.shard_map(
        body,
        mesh=mesh,
        in_specs=placed,
        out_specs=(
            P("dp", "seq", None),
            P("dp", "seq", None),
            P("dp", None),
            P(("dp", "seq")),
            P(("dp", "seq")),
            P(None, ("dp", "seq")),
            P(("dp", "seq")),
            P(("dp", "seq"), None),
            P(("dp", "seq"), None),
            P(("dp", "seq"), None),
            P(("dp", "seq")),
            P(("dp", "seq"), None),
            P(("dp", "seq")),
        ),
        check_vma=False,
    )
```

profile of v0, /device:TPU:0, one launch (start us, length us, event | category | flops | bytes accessed | tf_op | source)
XLA Modules:
  0.0 1435.0 jit_solution(18251976575772856435)
XLA Ops:
  21.4 8.4 fusion.135
  53.6 82.2 %all-gather.9.cloned.1.call-done = bf16[3,1024,12,64]{1,3,2,0:T(8,128)(2,1)} async-done(((bf16[3,256,12,64]{1,3,2,0:T(8,128)(2,1)}), bf16[3,1024,12,64]{1,3,2,0:T(8,128)(2,1)}) %all-gather.9.cloned.1.call-update) | async-done | bytes 4718608 | tf_op jit(solution)/shard_map/all_gather | solution.py:195
  135.8 89.5 %all-gather.13.cloned.1.call-done = bf16[3,1024,1,12,64]{1,4,3,2,0:T(8,128)(2,1)} async-done(((bf16[3,256,1,12,64]{1,4,3,2,0:T(8,128)(2,1)}), bf16[3,1024,1,12,64]{1,4,3,2,0:T(8,128)(2,1)}) %all-gather.13.cloned.1.call-update) | async-done | bytes 4718608 | tf_op jit(solution)/shard_map/all_gather | solution.py:196
  225.4 39.2 %while.37 = (s32[]{:T(128)}, bf16[3,256,12,64]{1,3,2,0:T(8,128)(2,1)S(1)}, f32[3,12,256]{2,1,0:T(8,128)}, bf16[3,1024,12,64]{1,3,2,0:T(8,128)(2,1)}, s32[3]{0:T(...) while((s32[]{:T(128)}, ...), condition=%wide.region_13.14_spmd, body=%wide.region_10.13_spmd.sunk | while | flops 843249664 | bytes 41797744 | solution.py:65
  264.6 50.2 %all-gather.11.cloned.1.call-done = bf16[3,1024,1,12,64]{1,4,3,2,0:T(8,128)(2,1)} async-done(((bf16[3,256,1,12,64]{1,4,3,2,0:T(8,128)(2,1)}), bf16[3,1024,1,12,64]{1,4,3,2,0:T(8,128)(2,1)}) %all-gather.11.cloned.1.call-update) | async-done | bytes 4718608 | tf_op jit(solution)/shard_map/all_gather | solution.py:186
  314.8 88.8 %all-gather.7.cloned.1.call-done = bf16[3,1024,12,64]{1,3,2,0:T(8,128)(2,1)} async-done(((bf16[3,256,12,64]{1,3,2,0:T(8,128)(2,1)}), bf16[3,1024,12,64]{1,3,2,0:T(8,128)(2,1)}) %all-gather.7.cloned.1.call-update) | async-done | bytes 4718608 | tf_op jit(solution)/shard_map/all_gather | solution.py:185
  404.7 57.4 %while.36 = (s32[]{:T(128)}, bf16[3,256,12,64]{1,3,2,0:T(8,128)(2,1)}, bf16[3,1024,12,64]{1,3,2,0:T(8,128)(2,1)}, s32[3]{0:T(128)S(1)}, bf16[3,256,12,64]{1,3,2,...) while((s32[]{:T(128)}, bf16[3,256,12,64]{1,3,2,0:T(8,128)(2,1)}, ...), condition=%wide.region_5.6_spmd, body=%wide.region_2.5_spmd.sunk | while | flops 830670848 | bytes 54292580 | solution.py:65
  409.3 6.6 fusion.220
  415.9 7.9 fusion.221
  435.1 7.9 fusion.221
  454.2 7.9 fusion.221
  480.2 13.4 convolution_add_fusion.2
  493.6 12.4 convolution_add_fusion.1
  508.5 12.1 convert_reduce_fusion
  546.5 92.4 %while.38 = (s32[]{:T(128)}, f32[3,256,12,64]{1,3,2,0:T(8,128)}, bf16[3,1024,12,64]{1,3,2,0:T(8,128)(2,1)}, bf16[3,1024,12,64]{1,3,2,0:T(8,128)(2,1)}, bf16[3,10...) while((s32[]{:T(128)}, f32[3,256,12,64]{1,3,2,0:T(8,128)}, ...), condition=%wide.region_20.21_spmd, body=%wide.region_18.20_spmd.sunk | while | flops 2061432832 | bytes 107844744 | solution.py:93
  555.5 8.4 multiply_reduce_fusion.8
  564.0 6.6 multiply_convert_fusion.6
  586.4 8.4 multiply_reduce_fusion.8
  594.8 6.6 multiply_convert_fusion.6
  617.2 8.4 multiply_reduce_fusion.8
  625.6 6.6 multiply_convert_fusion.6
  645.4 13.2 fusion.152
  659.9 8.6 fusion.163
  668.7 53.9 %reduce-scatter.8.cloned.1.call-done = bf16[3,256,12,64]{1,3,2,0:T(8,128)(2,1)} async-done(((bf16[3,1024,12,64]{1,3,2,0:T(8,128)(2,1)}), bf16[3,256,12,64]{1,3,2,0:T(8,128)(2,1)}) %reduce-scatter.8.cloned.1.call-update) | async-done | bytes 1179664 | tf_op jit(solution)/shard_map/reduce_scatter | solution.py:252
  725.1 85.4 %reduce-scatter.10.cloned.1.call-done = bf16[3,256,12,64]{1,3,2,0:T(8,128)(2,1)} async-done(((bf16[3,1024,12,64]{1,3,2,0:T(8,128)(2,1)}), bf16[3,256,12,64]{1,3,2,0:T(8,128)(2,1)}) %reduce-scatter.10.cloned.1.call-update) | async-done | bytes 1179664 | tf_op jit(solution)/shard_map/reduce_scatter | solution.py:255
  839.5 42.6 %all-reduce.5 = (f32[768]{0:T(1024)}, f32[768]{0:T(1024)}, f32[4608]{0:T(1024)}, f32[3072]{0:T(1024)}, f32[768]{0:T(1024)}) all-reduce(f32[768]{0:T(1024)} %get-tuple-element.186, f32[768]{0:T(1024)} %get-tuple-element.183, f32[4608]{0:T(1024)} %reduce_sum.254, ...), channel_id=6, replica_groups=mesh['dp'=8,'seq'=4] {'dp','seq'}, use_global_device_ids=true, to_apply=%region_33.34.clone | all-reduce | flops 9984 | bytes 79872
  891.0 11.3 psum.7
  907.5 8.5 reduce-scatter.16.cloned.1.call-done
  916.0 142.0 %reduce-scatter.20.cloned.1.call-done = f32[96,768]{1,0:T(8,128)} async-done(((f32[3072,768]{1,0:T(8,128)}), f32[96,768]{1,0:T(8,128)}) %reduce-scatter.20.cloned.1.call-update) | async-done | bytes 294928 | tf_op jit(solution)/shard_map/reduce_scatter | solution.py:303
  1058.0 141.1 %reduce-scatter.18.cloned.1.call-done = f32[24,3072]{1,0:T(8,128)} async-done(((f32[768,3072]{1,0:T(8,128)}), f32[24,3072]{1,0:T(8,128)}) %reduce-scatter.18.cloned.1.call-update) | async-done | bytes 294928 | tf_op jit(solution)/shard_map/reduce_scatter | solution.py:301
  1199.1 104.7 %reduce-scatter.12.cloned.1.call-done = f32[128,144]{0,1:T(8,128)} async-done(((f32[128,4608]{0,1:T(8,128)}), f32[128,144]{0,1:T(8,128)}) %reduce-scatter.12.cloned.1.call-update) | async-done | bytes 73744 | tf_op jit(solution)/shard_map/reduce_scatter | solution.py:297
  1303.8 124.4 %reduce-scatter.14.cloned.1.call-done = f32[24,2304]{1,0:T(8,128)} async-done(((f32[768,2304]{1,0:T(8,128)}), f32[24,2304]{1,0:T(8,128)}) %reduce-scatter.14.cloned.1.call-update) | async-done | bytes 221200 | tf_op jit(solution)/shard_map/reduce_scatter | solution.py:299
  (303 shorter events, 251.8 us)
Async XLA Ops:
  7.2 454.9 %copy-start = (bf16[768,768]{1,0:T(8,128)(2,1)S(1)}, bf16[768,768]{1,0:T(8,128)(2,1)}, u32[]{:S(2)}) copy-start(bf16[768,768]{1,0:T(8,128)(2,1)} %param.28) | copy-start | bytes 3538948
  7.2 128.6 %all-gather.9.cloned.1.call-start = ((), (), s32[]{:S(2)}) async-start(), calls=%async_computation.8 | async-start | bytes 5898240 | tf_op jit(solution)/shard_map/all_gather | solution.py:195
  11.5 8.9 copy-start.41
  12.0 8.5 copy-start.54
  21.3 8.5 copy-start.27
  21.4 8.4 copy-start.24
  43.8 181.5 %all-gather.13.cloned.1.call-start = ((), (), s32[]{:S(2)}) async-start(), calls=%async_computation.17 | async-start | bytes 5898240 | tf_op jit(solution)/shard_map/all_gather | solution.py:196
  46.7 268.0 %all-gather.11.cloned.1.call-start = ((), (), s32[]{:S(2)}) async-start(), calls=%async_computation.16 | async-start | bytes 5898240 | tf_op jit(solution)/shard_map/all_gather | solution.py:186
  49.7 353.9 %all-gather.7.cloned.1.call-start = ((), (), s32[]{:S(2)}) async-start(), calls=%async_computation.7 | async-start | bytes 5898240 | tf_op jit(solution)/shard_map/all_gather | solution.py:185
  50.9 671.7 %reduce-scatter.8.cloned.1.call-start = ((), (), s32[]{:S(2)}) async-start(), calls=%async_computation.9 | async-start | bytes 5898240 | tf_op jit(solution)/shard_map/reduce_scatter | solution.py:252
  52.5 172.9 %copy-start.66 = (s32[3]{0:T(128)S(1)}, s32[3]{0:T(128)}, u32[]{:S(2)}) copy-start(s32[3]{0:T(128)} %param.22) | copy-start | bytes 40
  264.6 140.1 %copy-start.5 = (bf16[3,256,12,64]{1,3,2,0:T(8,128)(2,1)}, bf16[3,256,12,64]{1,3,2,0:T(8,128)(2,1)S(1)}, u32[]{:S(2)}) copy-start(bf16[3,256,12,64]{1,3,2,0:T(8,128)(2,1)S(1)} %get-tuple-element.546) | copy-start | bytes 3538948
  264.6 140.1 %copy-start.11 = (bf16[3,256,12,64]{1,3,2,0:T(8,128)(2,1)}, bf16[3,256,12,64]{1,3,2,0:T(8,128)(2,1)S(1)}, u32[]{:S(2)}) copy-start(bf16[3,256,12,64]{1,3,2,0:T(8,128)(2,1)S(1)} %get-tuple-element.138) | copy-start | bytes 3538948
  404.7 57.4 %copy-start.2 = (bf16[3,256,768]{2,1,0:T(8,128)(2,1)S(1)}, bf16[3,256,768]{2,1,0:T(8,128)(2,1)}, u32[]{:S(2)}) copy-start(bf16[3,256,768]{2,1,0:T(8,128)(2,1)} %param.20) | copy-start | bytes 3538948
  404.7 57.4 %copy-start.39 = (f32[3,768]{1,0:T(4,128)S(1)}, f32[3,768]{1,0:T(4,128)}, u32[]{:S(2)}) copy-start(f32[3,768]{1,0:T(4,128)} %get-tuple-element.279) | copy-start | bytes 27652
  493.6 12.5 copy-start.10
  493.6 12.5 copy-start.20
  493.6 12.5 copy-start.26
  493.6 12.5 copy-start.49
  493.6 14.9 %copy-start.69 = (f32[768,3072]{1,0:T(8,128)S(1)}, f32[768,3072]{1,0:T(8,128)}, u32[]{:S(2)}) copy-start(f32[768,3072]{1,0:T(8,128)} %fusion.159) | copy-start | bytes 28311556
  506.1 14.5 %slice-start.2 = ((s8[4718592]{0:T(1024)(128)(4,1)}), s8[4194304]{0:T(1024)(128)(4,1)S(1)}, s32[]{:S(2)}) async-start(s8[4718592]{0:T(1024)(128)(4,1)} %bitcast.284), calls=%async_computation.20 | async-start | bytes 8388608
  508.4 12.1 copy-start.29
  508.4 12.1 copy-start.52
  508.5 12.1 slice-start.3
  638.9 171.6 %reduce-scatter.10.cloned.1.call-start = ((), (), s32[]{:S(2)}) async-start(), calls=%async_computation.10 | async-start | bytes 5898240 | tf_op jit(solution)/shard_map/reduce_scatter | solution.py:255
  639.5 276.4 %reduce-scatter.16.cloned.1.call-start = ((), (), s32[]{:S(2)}) async-start(), calls=%async_computation.13 | async-start | bytes 2433024 | tf_op jit(solution)/shard_map/reduce_scatter | solution.py:300
  644.1 413.9 %reduce-scatter.20.cloned.1.call-start = ((), (), s32[]{:S(2)}) async-start(), calls=%async_computation.15 | async-start | bytes 9732096 | tf_op jit(solution)/shard_map/reduce_scatter | solution.py:303
  658.6 540.5 %reduce-scatter.18.cloned.1.call-start = ((), (), s32[]{:S(2)}) async-start(), calls=%async_computation.14 | async-start | bytes 9732096 | tf_op jit(solution)/shard_map/reduce_scatter | solution.py:301
  668.5 55.7 %copy-start.25 = (f32[3,256,12,64]{1,3,2,0:T(8,128)S(1)}, f32[3,256,12,64]{1,3,2,0:T(8,128)}, u32[]{:S(2)}) copy-start(f32[3,256,12,64]{1,3,2,0:T(8,128)} %get-tuple-element.140) | copy-start | bytes 7077892
  668.5 635.4 %reduce-scatter.12.cloned.1.call-start = ((), (), s32[]{:S(2)}) async-start(), calls=%async_computation.11 | async-start | bytes 2433024 | tf_op jit(solution)/shard_map/reduce_scatter | solution.py:297
  825.8 602.5 %reduce-scatter.14.cloned.1.call-start = ((), (), s32[]{:S(2)}) async-start(), calls=%async_computation.12 | async-start | bytes 7299072 | tf_op jit(solution)/shard_map/reduce_scatter | solution.py:299
  837.8 50.6 %copy-start.18 = (bf16[128,4608]{1,0:T(8,128)(2,1)S(1)}, bf16[128,4608]{1,0:T(8,128)(2,1)}, u32[]{:S(2)}) copy-start(bf16[128,4608]{1,0:T(8,128)(2,1)} %param.25) | copy-start | bytes 3538948
  (53 other events, 184.8 us)
Sparse Core Ops, SparseCore 0:
  43.9 91.8 all-gather.8
  137.9 87.3 all-gather.12
  227.4 87.3 all-gather.10
  316.2 87.3 all-gather.6
  639.1 83.4 reduce-scatter.7
  724.7 85.7 reduce-scatter.9
  816.4 99.5 reduce-scatter.15
  923.4 134.5 reduce-scatter.19
  1064.5 134.5 reduce-scatter.17
  1205.7 98.1 reduce-scatter.11
  1310.1 118.1 reduce-scatter.13
where the time goes:
time: 1440 us
  waiting for transfers between devices  971 us (67%)
  matrix products  237 us (16%)
  other arithmetic  98 us (7%)
  local copies, waits for them, and re-layouts  58.7 us (4%)
  blocking collectives  53.9 us (4%)
  between operations  14.9 us (1%)
    all_gather x2, waiting for transfers between devices, body(): lax.all_gather(early_part[6], 'seq', axis=1, tiled=True)  171 us
    reduce_scatter x1, waiting for transfers between devices, body(): lax.psum_scatter(grad_w_down, ('dp', 'seq'), scatter_dimension=0, tiled=T...  142 us
    reduce_scatter x1, waiting for transfers between devices, body(): lax.psum_scatter(grad_w_up, ('dp', 'seq'), scatter_dimension=0, tiled=True)  141 us
    all_gather x2, waiting for transfers between devices, body(): lax.all_gather(early_part[7], 'seq', axis=1, tiled=True)  140 us
    reduce_scatter x1, waiting for transfers between devices, body(): lax.psum_scatter(grad_w_qkv, ('dp', 'seq'), scatter_dimension=0, tiled=True)  124 us
    reduce_scatter x1, waiting for transfers between devices, body(): lax.psum_scatter(grad_w_ada, ('dp', 'seq'), scatter_dimension=1, tiled=True)  105 us
    reduce_scatter x1, waiting for transfers between devices, body(): lax.psum_scatter(grad_values_all.astype(jnp.bfloat16), 'seq', scatter_dim...  85.4 us
    reduce_scatter x1, waiting for transfers between devices, body(): lax.psum_scatter(grad_keys_all.astype(jnp.bfloat16), 'seq', scatter_dimen...  53.9 us
  transfers between devices with their start and end apart: 11, of which 11 were waited for; matrix products, arithmetic and copies ran while one was open for 8% of the time, Pallas kernels for 0%

commit v1 on v0

v1 whole, which is shorter than its diff:
```python
import functools

import jax
import jax.numpy as jnp
import numpy as np
from jax import lax
from jax.experimental import pallas as pl
from jax.experimental.pallas import tpu as pltpu
from jax.sharding import PartitionSpec as P

HEADS = 12
HD = 64
EPS = 1e-05
HIGH = lax.Precision.HIGHEST
BF = jnp.bfloat16
F32 = jnp.float32
PACK = 4
BLOCK = PACK * HD
HALF = BLOCK // 2
SPANS = (128, 512, 1024)
GELU_C = float(np.sqrt(2.0 / np.pi))


def nn(left, right):
    return lax.dot_general(left, right, (((1,), (0,)), ((), ())), preferred_element_type=F32)


def nt(left, right):
    return lax.dot_general(left, right, (((1,), (1,)), ((), ())), preferred_element_type=F32)


def normalize(vector):
    average = jnp.mean(vector, axis=-1, keepdims=True)
    centred = vector - average
    inverse = lax.rsqrt(jnp.mean(centred * centred, axis=-1, keepdims=True) + EPS)
    return centred * inverse, inverse


def norm_back(grad_normed, normed, inverse):
    return inverse * (
        grad_normed
        - jnp.mean(grad_normed, axis=-1, keepdims=True)
        - normed * jnp.mean(grad_normed * normed, axis=-1, keepdims=True)
    )


def rows_sum(value):
    return jnp.sum(value, axis=0, keepdims=True)


def head_masks():
    lane = lax.broadcasted_iota(jnp.int32, (1, BLOCK), 1)
    split = [((lane % HALF) // (HD // 2) == h).astype(F32).astype(BF) for h in range(PACK)]
    plain = [(lane // HD == h).astype(F32).astype(BF) for h in range(PACK)]
    return split, plain


def prep_kernel(
    place, near_ref, far_ref, mod_ref, gain_ref, wq_ref, wk_ref, wv_ref, cos_ref, sin_ref,
    actt_ref, q_ref, k_ref, v_ref,
):
    step = pl.program_id(0)
    rows = near_ref.shape[1]
    source = jnp.where(step < 2, near_ref[0], far_ref[0]).astype(F32)
    normed, _ = normalize(source)
    act = (normed * gain_ref[...] * (1.0 + mod_ref[0, 1:2, :]) + mod_ref[0, 0:1, :]).astype(BF)
    actt_ref[...] = act.T
    cosine, sine = cos_ref[...], sin_ref[...]

    def turned(weight_ref, out_ref, factor):
        for block in range(weight_ref.shape[1] // BLOCK):
            at = block * BLOCK
            both = nn(act, weight_ref[:, at : at + BLOCK])
            front, back = both[:, :HALF], both[:, HALF:]
            out_ref[:, at : at + HALF] = (front * cosine - back * sine).astype(BF) * factor
            out_ref[:, at + HALF : at + BLOCK] = (back * cosine + front * sine).astype(BF) * factor

    @pl.when((place[0] ^ step) * rows < place[1])
    def _():
        turned(wk_ref, k_ref, BF(1.0))
        v_ref[...] = nn(act, wv_ref[...]).astype(BF)

    @pl.when(step == 0)
    def _():
        turned(wq_ref, q_ref, BF(HD**-0.5))


def attend_kernel(place, q_ref, k_ref, v_ref, mix_ref, lse_ref):
    split, plain = head_masks()
    lane = lax.broadcasted_iota(jnp.int32, (1, BLOCK), 1)
    narrow = lax.broadcasted_iota(jnp.int32, (1, 128), 1)

    def work(span):
        queries, keys, values = q_ref[...], k_ref[:span, :], v_ref[:span, :]
        mixed = jnp.zeros(q_ref.shape, F32)
        logs = jnp.zeros((q_ref.shape[0], 128), F32)
        for head in range(PACK):
            scores = nt(queries * split[head], keys)
            top = jnp.max(scores, axis=-1, keepdims=True)
            raised = jnp.exp(scores - top)
            total = jnp.sum(raised, axis=-1, keepdims=True)
            probs = (raised * (1.0 / total)).astype(BF)
            mixed = jnp.where(lane // HD == head, nn(probs, values), mixed)
            logs = jnp.where(narrow == head, top + jnp.log(total), logs)
        mix_ref[...] = mixed.astype(BF)
        lse_ref[0] = logs.T[:8, :]

    for span in SPANS:
        pl.when(place[1] == span)(functools.partial(work, span))


def attend_back_kernel(
    place, q_ref, k_ref, v_ref, g_ref, lse_ref, cosq_ref, sinq_ref, cosk_ref, sink_ref,
    dq_ref, dk_ref, dv_ref,
):
    split, plain = head_masks()
    part = HD // 2

    def unturn(both, cosine, sine, out_ref, span):
        front, back = both[:, :HALF], both[:, HALF:]
        out_ref[:span, :HALF] = (front * cosine + back * sine).astype(BF)
        out_ref[:span, HALF:] = (back * cosine - front * sine).astype(BF)

    def work(span):
        queries, grads = q_ref[...], g_ref[...]
        keys, values = k_ref[:span, :], v_ref[:span, :]
        keys_t = keys.T
        grad_keys = jnp.zeros((span, BLOCK), F32)
        grad_values = jnp.zeros((span, BLOCK), F32)
        fronts, backs = [], []
        for head in range(PACK):
            query, grad = queries * split[head], grads * plain[head]
            probs = jnp.exp(nt(keys, query) - lse_ref[0, head : head + 1, :])
            grad_probs = nt(values, grad)
            inner = rows_sum(probs * grad_probs)
            grad_scores = (probs * (grad_probs - inner)).astype(BF)
            grad_values = grad_values + nn(probs.astype(BF), grad)
            grad_keys = grad_keys + nn(grad_scores, query)
            at = head * part
            rows_t = jnp.concatenate(
                [keys_t[at : at + part], keys_t[HALF + at : HALF + at + part]], axis=0
            )
            grad_query = nn(rows_t, grad_scores)
            fronts.append(grad_query[:part])
            backs.append(grad_query[part:])
        grad_queries = jnp.concatenate(fronts + backs, axis=0).T * HD**-0.5
        unturn(grad_queries, cosq_ref[...], sinq_ref[...], dq_ref, dq_ref.shape[0])
        unturn(grad_keys, cosk_ref[:span, :], sink_ref[:span, :], dk_ref, span)
        dv_ref[:span, :] = grad_values.astype(BF)
        rest = dk_ref.shape[0] - span
        if rest:
            dk_ref[span:, :] = jnp.zeros((rest, BLOCK), BF)
            dv_ref[span:, :] = jnp.zeros((rest, BLOCK), BF)

    for span in SPANS:
        pl.when(place[1] == span)(functools.partial(work, span))


def mlp_kernel(
    mix0_ref, mix1_ref, mix2_ref, tok_ref, cot_ref, mod_ref, gain_ref, wout_ref, bdown_ref,
    wup_ref, bup_ref, wdown_ref,
    out_ref, gres_ref, gmix_ref, dwout_ref, sums_ref, dwup_ref, dwdown_ref, dbup_ref,
    resid, branch, act, act_t, slope, active, second, gsecond, gact, gpre,
):
    step = pl.program_id(0)
    tiles = pl.num_programs(0) // 2
    parts, rows, _ = tok_ref.shape
    mixes = (mix0_ref, mix1_ref, mix2_ref)

    def span(s):
        return slice(s * rows, (s + 1) * rows)

    def mod(s, which):
        return mod_ref[s, which : which + 1, :]

    @pl.when(step == 0)
    def _():
        for s in range(parts):
            one = nn(mixes[s][...], wout_ref[...])
            res = tok_ref[s].astype(F32) + mod(s, 2) * one
            branch[span(s), :] = one
            resid[span(s), :] = res
            normed, _ = normalize(res)
            value = (normed * gain_ref[...] * (1.0 + mod(s, 4)) + mod(s, 3)).astype(BF)
            act[span(s), :] = value
            act_t[:, span(s)] = value.T
            second[span(s), :] = jnp.zeros_like(res)
            gact[span(s), :] = jnp.zeros_like(res)

    @pl.when(step < tiles)
    def _():
        for s in range(parts):
            u = nn(act[span(s), :], wup_ref[...]) + bup_ref[...]
            square = u * u
            bent = jnp.tanh(GELU_C * (u + 0.044715 * (square * u)))
            value = (0.5 * u * (1.0 + bent)).astype(BF)
            slope[step, span(s), :] = 0.5 * (1.0 + bent) + 0.5 * u * (1.0 - bent * bent) * (
                GELU_C * (1.0 + 3 * 0.044715 * square)
            )
            active[step, span(s), :] = value
            second[span(s), :] += nn(value, wdown_ref[...])

    @pl.when(step == tiles - 1)
    def _():
        total = jnp.zeros(bdown_ref.shape, F32)
        for s in range(parts):
            two = second[span(s), :] + bdown_ref[...]
            out_ref[s] = (resid[span(s), :] + mod(s, 5) * two).astype(BF)
            pull = cot_ref[s].astype(F32)
            sums_ref[5 * parts + s : 5 * parts + s + 1, :] = rows_sum(pull * two)
            down = (pull * mod(s, 5)).astype(BF)
            gsecond[span(s), :] = down
            total = total + rows_sum(down.astype(F32))
        sums_ref[6 * parts : 6 * parts + 1, :] = total

    @pl.when(step >= tiles)
    def _():
        at = step - tiles
        total = jnp.zeros(bup_ref.shape, F32)
        for s in range(parts):
            pulled = nt(gsecond[span(s), :], wdown_ref[...])
            value = (pulled * slope[at, span(s), :]).astype(BF)
            gpre[span(s), :] = value
            total = total + rows_sum(value.astype(F32))
            gact[span(s), :] += nt(value, wup_ref[...])
        dbup_ref[...] = total
        dwdown_ref[...] = nn(active[at].T, gsecond[...])
        dwup_ref[...] = nn(act_t[...], gpre[...])

    @pl.when(step == 2 * tiles - 1)
    def _():
        total = jnp.zeros(bdown_ref.shape, F32)
        for s in range(parts):
            normed, inverse = normalize(resid[span(s), :])
            pull = gact[span(s), :]
            sums_ref[3 * parts + s : 3 * parts + s + 1, :] = rows_sum(pull)
            sums_ref[4 * parts + s : 4 * parts + s + 1, :] = rows_sum(
                pull * (normed * gain_ref[...])
            )
            scaled = pull * (1.0 + mod(s, 4))
            total = total + rows_sum(scaled * normed)
            grad = cot_ref[s].astype(F32) + norm_back(scaled * gain_ref[...], normed, inverse)
            gres_ref[s] = grad
            sums_ref[2 * parts + s : 2 * parts + s + 1, :] = rows_sum(grad * branch[span(s), :])
            one = (grad * mod(s, 2)).astype(BF)
            gmix_ref[s] = nt(one, wout_ref[...]).astype(BF)
            outer = nn(mixes[s][...].T, one)
            if s == 0:
                dwout_ref[...] = outer
            else:
                dwout_ref[...] += outer
        sums_ref[6 * parts + 1 : 6 * parts + 2, :] = total


def whole(array):
    rank = array.ndim
    return pl.BlockSpec(array.shape, lambda *_: (0,) * rank, pipeline_mode=pl.Buffered(1))


def limits(mib):
    return pltpu.CompilerParams(vmem_limit_bytes=mib * 2**20)


def cost(flops, bytes_accessed):
    return pl.CostEstimate(flops=int(flops), bytes_accessed=int(bytes_accessed), transcendentals=0)


def prepare(place, near, far, mod, s, gain, wq, wk, wv, cosine, sine):
    _, rows, width = near.shape
    slots = 4 * rows
    table = pl.BlockSpec((rows, HALF), lambda i, p: (p[0] ^ i, 0))
    piece = pl.BlockSpec((rows, width), lambda i, p: (p[0] ^ i, 0))
    return pl.pallas_call(
        prep_kernel,
        grid_spec=pltpu.PrefetchScalarGridSpec(
            num_scalar_prefetch=1,
            grid=(4,),
            in_specs=[
                pl.BlockSpec((1, rows, width), lambda i, p: (jnp.minimum(i, 1), 0, 0)),
                pl.BlockSpec((1, rows, width), lambda i, p: (jnp.maximum(i - 2, 0), 0, 0)),
                pl.BlockSpec((1,) + mod.shape[1:], lambda i, p: (s, 0, 0)),
                whole(gain), whole(wq), whole(wk), whole(wv), table, table,
            ],
            out_specs=[
                pl.BlockSpec((width, rows), lambda i, p: (0, p[0] ^ i)),
                pl.BlockSpec((rows, width), lambda i, p: (0, 0)),
                piece, piece,
            ],
        ),
        out_shape=[
            jax.ShapeDtypeStruct((width, slots), BF),
            jax.ShapeDtypeStruct((rows, width), BF),
            jax.ShapeDtypeStruct((slots, width), BF),
            jax.ShapeDtypeStruct((slots, width), BF),
        ],
        compiler_params=limits(40),
        cost_estimate=cost(2 * slots * width * width * 2.25, 10e6),
    )(place, near, far, mod, gain, wq, wk, wv, cosine, sine)


def attend(place, queries, keys, values):
    rows, width = queries.shape
    slots = keys.shape[0]
    groups = width // BLOCK
    own = pl.BlockSpec((rows, BLOCK), lambda j, p: (0, j))
    full = pl.BlockSpec((slots, BLOCK), lambda j, p: (0, j))
    return pl.pallas_call(
        attend_kernel,
        grid_spec=pltpu.PrefetchScalarGridSpec(
            num_scalar_prefetch=1,
            grid=(groups,),
            in_specs=[own, full, full],
            out_specs=[own, pl.BlockSpec((1, 8, rows), lambda j, p: (j, 0, 0))],
        ),
        out_shape=[
            jax.ShapeDtypeStruct((rows, width), BF),
            jax.ShapeDtypeStruct((groups, 8, rows), F32),
        ],
        compiler_params=limits(40),
        cost_estimate=cost(16 * rows * slots * width, 5e6),
    )(place, queries, keys, values)


def attend_back(place, queries, keys, values, grads, s, logs, cosine, sine):
    rows, width = queries.shape
    slots = keys.shape[0]
    groups = width // BLOCK
    own = pl.BlockSpec((rows, BLOCK), lambda j, p: (0, j))
    full = pl.BlockSpec((slots, BLOCK), lambda j, p: (0, j))
    own_table = pl.BlockSpec((rows, HALF), lambda j, p: (p[0], 0))
    full_table = pl.BlockSpec((slots, HALF), lambda j, p: (0, 0))
    return pl.pallas_call(
        attend_back_kernel,
        grid_spec=pltpu.PrefetchScalarGridSpec(
            num_scalar_prefetch=1,
            grid=(groups,),
            in_specs=[
                own, full, full,
                pl.BlockSpec((None, rows, BLOCK), lambda j, p: (s, 0, j)),
                pl.BlockSpec((1, 8, rows), lambda j, p: (j, 0, 0)),
                own_table, own_table, full_table, full_table,
            ],
            out_specs=[own, full, full],
        ),
        out_shape=[
            jax.ShapeDtypeStruct((rows, width), BF),
            jax.ShapeDtypeStruct((slots, width), BF),
            jax.ShapeDtypeStruct((slots, width), BF),
        ],
        compiler_params=limits(48),
        cost_estimate=cost(40 * rows * slots * width, 9e6),
    )(place, queries, keys, values, grads, logs, cosine, sine, cosine, sine)


def feed_forward(mixes, tokens, pulls, mod, gain, w_out, b_down, w_up, b_up, w_down):
    parts, rows, width = tokens.shape
    hidden = w_up.shape[1]
    tile = 512
    tiles = hidden // tile
    total = parts * rows
    late = lambda i: jnp.maximum(i - tiles, 0)
    wide = pl.BlockSpec((width, tile), lambda i: (0, i % tiles))
    bias = pl.BlockSpec((1, tile), lambda i: (0, i % tiles))
    tall = pl.BlockSpec((tile, width), lambda i: (i % tiles, 0))
    outs = [
        jax.ShapeDtypeStruct(tokens.shape, BF),
        jax.ShapeDtypeStruct(tokens.shape, F32),
        jax.ShapeDtypeStruct(tokens.shape, BF),
        jax.ShapeDtypeStruct((width, width), F32),
        jax.ShapeDtypeStruct((24, width), F32),
        jax.ShapeDtypeStruct((width, hidden), F32),
        jax.ShapeDtypeStruct((hidden, width), F32),
        jax.ShapeDtypeStruct((1, hidden), F32),
    ]
    return pl.pallas_call(
        mlp_kernel,
        grid=(2 * tiles,),
        in_specs=[whole(m) for m in mixes]
        + [whole(a) for a in (tokens, pulls, mod, gain, w_out, b_down)]
        + [wide, bias, tall],
        out_specs=[whole(o) for o in outs[:5]]
        + [
            pl.BlockSpec((width, tile), lambda i: (0, late(i))),
            pl.BlockSpec((tile, width), lambda i: (late(i), 0)),
            pl.BlockSpec((1, tile), lambda i: (0, late(i))),
        ],
        out_shape=outs,
        scratch_shapes=[
            pltpu.VMEM((total, width), F32),
            pltpu.VMEM((total, width), F32),
            pltpu.VMEM((total, width), BF),
            pltpu.VMEM((width, total), BF),
            pltpu.VMEM((tiles, total, tile), F32),
            pltpu.VMEM((tiles, total, tile), BF),
            pltpu.VMEM((total, width), F32),
            pltpu.VMEM((total, width), BF),
            pltpu.VMEM((total, width), F32),
            pltpu.VMEM((total, tile), BF),
        ],
        compiler_params=limits(60),
        cost_estimate=cost(2 * total * width * (6 * hidden + 3 * width), 50e6),
    )(*mixes, tokens, pulls, mod, gain, w_out, b_down, w_up, b_up, w_down)


def split_halves(weight):
    depth, width = weight.shape
    return (
        weight.reshape(depth, width // BLOCK, PACK, 2, HD // 2)
        .transpose(0, 1, 3, 2, 4)
        .reshape(depth, width)
    )


def join_halves(weight):
    depth, width = weight.shape
    return (
        weight.reshape(depth, width // BLOCK, 2, PACK, HD // 2)
        .transpose(0, 1, 3, 2, 4)
        .reshape(depth, width)
    )


def body(
    dp_size, seq_size,
    tokens, cond, lengths, gain_one, gain_two, w_ada, b_ada, w_qkv, w_out, w_up, b_up, w_down,
    b_down, cotangent,
):
    parts, rows, width = tokens.shape
    hidden = w_up.shape[1]
    slots = rows * seq_size
    dp_bits = dp_size.bit_length() - 1
    dp, seq = lax.axis_index("dp"), lax.axis_index("seq")
    core, side = dp & 1, seq // (seq_size // 2)
    stays = core == side
    own = jnp.where(stays, seq, seq ^ 2).astype(jnp.int32)

    def dp_swap(value, bit):
        return lax.ppermute(value, "dp", [(i, i ^ (1 << bit)) for i in range(dp_size)])

    def seq_swap(value, bit):
        return lax.ppermute(value, "seq", [(i, i ^ bit) for i in range(seq_size)])

    pairs = []
    for i in range(dp_size):
        for j in range(seq_size):
            if (i & 1) != j // (seq_size // 2):
                pairs.append((i * seq_size + j, (i ^ 1) * seq_size + (j ^ 2)))

    def regroup(value):
        moved = lax.ppermute(value, ("dp", "seq"), pairs)
        return jnp.where(stays, value, moved)

    cond_here = jnp.where(stays, cond, dp_swap(cond, 0))
    lengths_here = jnp.where(stays, lengths, dp_swap(lengths, 0))
    mod = jnp.dot(cond_here, w_ada, preferred_element_type=F32) + b_ada
    mod = mod.reshape(parts, 6, width)
    places = [jnp.stack([own, lengths_here[s]]).astype(jnp.int32) for s in range(parts)]
    frequency = np.power(10000.0, -np.arange(HD // 2) * 2.0 / HD).astype(np.float32)
    angles = jnp.arange(slots).astype(F32)[:, None] * jnp.asarray(frequency)[None, :]
    cosine = jnp.tile(jnp.cos(angles), (1, PACK))
    sine = jnp.tile(jnp.sin(angles), (1, PACK))
    wq = split_halves(w_qkv[:, :width])
    wk = split_halves(w_qkv[:, width : 2 * width])
    wv = w_qkv[:, 2 * width :]
    gain_one_row, gain_two_row = gain_one[None, :], gain_two[None, :]

    tokens_here, nears, fars = [], [], []
    for s in range(parts):
        mine = regroup(tokens[s])
        near = jnp.stack([mine, seq_swap(mine, 1)])
        tokens_here.append(mine)
        nears.append(near)
        fars.append(dp_swap(near, 0))
    pulls = jnp.stack([regroup(cotangent[s]) for s in range(parts)])

    saved, mixes = [], []
    for s in range(parts):
        act_t, queries, keys, values = prepare(
            places[s], nears[s], fars[s], mod, s, gain_one_row, wq, wk, wv, cosine, sine
        )
        mixture, logs = attend(places[s], queries, keys, values)
        saved.append((act_t, queries, keys, values, logs))
        mixes.append(mixture)

    output, grad_res, grad_mix, dw_out, sums, dw_up, dw_down, db_up = feed_forward(
        mixes, jnp.stack(tokens_here), pulls, mod, gain_two_row, w_out, b_down[None, :],
        w_up, b_up[None, :], w_down,
    )
    output = regroup(output)

    def reduce_rows(weight, bits):
        columns = weight.shape[1]
        piece = weight.shape[0] // (dp_size * seq_size)
        held = weight.reshape((2,) * dp_bits + (2, 2, piece, columns))
        names = [("dp", b) for b in reversed(range(dp_bits))] + [("seq", 1), ("seq", 0)]
        for axis, bit in [("dp", b) for b in bits] + [("seq", 0), ("seq", 1)]:
            at = names.index((axis, bit))
            index = ((dp if axis == "dp" else seq) >> bit) & 1
            keep = lax.dynamic_index_in_dim(held, index, at, keepdims=False)
            send = lax.dynamic_index_in_dim(held, 1 - index, at, keepdims=False).astype(BF)
            got = dp_swap(send, bit) if axis == "dp" else seq_swap(send, 1 << bit)
            held = keep + got.astype(F32)
            names.pop(at)
        return held

    forth = list(range(dp_bits))
    back = [0] + list(reversed(range(1, dp_bits)))
    g_w_down = reduce_rows(dw_down, back)
    g_w_up = reduce_rows(dw_up, forth)
    g_w_out = reduce_rows(dw_out, back)

    grad_tokens, first = [], []
    dw_q = dw_k = dw_v = 0.0
    gain_sum = 0.0
    for s in range(parts):
        act_t, queries, keys, values, logs = saved[s]
        dq, dk, dv = attend_back(
            places[s], queries, keys, values, grad_mix, s, logs, cosine, sine
        )
        dw_q = dw_q + nn(lax.dynamic_slice_in_dim(act_t, own * rows, rows, 1), dq)
        dw_k = dw_k + nn(act_t, dk)
        dw_v = dw_v + nn(act_t, dv)
        share = (nt(dk, wk) + nt(dv, wv)).reshape(seq_size, rows, width)
        pick = lambda k: lax.dynamic_index_in_dim(share, own ^ k, 0, keepdims=False)
        send = jnp.stack([pick(2), pick(3)]).astype(BF)
        got = dp_swap(send, 0).astype(F32)
        here = pick(0) + nt(dq, wq) + got[0]
        there = (pick(1) + got[1]).astype(BF)
        grad_act = here + seq_swap(there, 1).astype(F32)
        source = tokens_here[s].astype(F32)
        normed, inverse = normalize(source)
        scaled = grad_act * (1.0 + mod[s, 1:2, :])
        shift_sum = rows_sum(grad_act)
        scale_sum = rows_sum(grad_act * (normed * gain_one_row))
        gain_sum = gain_sum + rows_sum(scaled * normed)
        first.append((shift_sum, scale_sum))
        grad = grad_res[s] + norm_back(scaled * gain_one_row, normed, inverse)
        moved = lax.ppermute(grad.astype(BF), ("dp", "seq"), pairs)
        grad_tokens.append(jnp.where(stays, grad, moved.astype(F32)))
    dw_qkv = jnp.concatenate([dw_q, dw_k, dw_v], axis=1)
    g_w_qkv = jnp.concatenate(
        [
            reduce_rows(dw_qkv[:, : 3 * width // 2], forth),
            reduce_rows(dw_qkv[:, 3 * width // 2 :], back),
        ],
        axis=1,
    )
    g_w_qkv = jnp.concatenate(
        [
            join_halves(g_w_qkv[:, :width]),
            join_halves(g_w_qkv[:, width : 2 * width]),
            g_w_qkv[:, 2 * width :],
        ],
        axis=1,
    )

    grad_mod = jnp.concatenate(
        [
            jnp.concatenate([f[0] for f in first]),
            jnp.concatenate([f[1] for f in first]),
            sums[2 * parts : 3 * parts],
            sums[3 * parts : 4 * parts],
            sums[4 * parts : 5 * parts],
            sums[5 * parts : 6 * parts],
        ],
        axis=1,
    )
    share = jnp.dot(grad_mod, w_ada.astype(F32).T, precision=HIGH)
    shards = dp_size * seq_size
    cut = lambda v: v.reshape((2,) * dp_bits + (2, 2, -1))
    held = jnp.concatenate(
        [cut(v) for v in (gain_sum, sums[6 * parts + 1], db_up, sums[6 * parts])], axis=-1
    )
    lanes = grad_mod.reshape(parts, shards, -1).transpose(1, 0, 2)
    per = lanes.shape[-1]
    lanes = lanes.reshape((2,) * dp_bits + (2, 2, parts, per))
    conds = cond_here.astype(F32)
    names = [("dp", b) for b in reversed(range(dp_bits))] + [("seq", 1), ("seq", 0)]
    order = [("dp", 0), ("seq", 0), ("seq", 1)] + [("dp", b) for b in range(1, dp_bits)]
    for turn, (axis, bit) in enumerate(order):
        at = names.index((axis, bit))
        index = ((dp if axis == "dp" else seq) >> bit) & 1
        swap = (lambda v: dp_swap(v, bit)) if axis == "dp" else (lambda v: seq_swap(v, 1 << bit))
        pick = lambda v, i: lax.dynamic_index_in_dim(v, i, at, keepdims=False)
        sent = [pick(held, 1 - index), pick(lanes, 1 - index)]
        if turn < 2:
            sent.append(share)
        elif turn == 2:
            sent += [share, conds]
        else:
            sent.append(conds)
        sizes = np.cumsum([v.size for v in sent])[:-1]
        got = swap(jnp.concatenate([v.reshape(-1) for v in sent]))
        got = [g.reshape(v.shape) for g, v in zip(jnp.split(got, sizes), sent)]
        held = pick(held, index) + got[0]
        mine = pick(lanes, index)
        if turn < 2:
            lanes = mine + got[1]
            share = share + got[2]
        else:
            lanes = jnp.concatenate([mine, got[1]], axis=-2)
            conds = jnp.concatenate([conds, got[-1]], axis=0)
            if turn == 2:
                share = jnp.where(stays, share, got[2])
        names.pop(at)
    sizes = np.cumsum([width // shards, width // shards, hidden // shards])
    g_gain_one, g_gain_two, g_b_up, g_b_down = jnp.split(held, sizes)
    g_w_ada = jnp.dot(conds.T, lanes, precision=HIGH)
    g_b_ada = jnp.sum(lanes, axis=0)
    return (
        output,
        jnp.stack(grad_tokens),
        share,
        g_gain_one,
        g_gain_two,
        g_w_ada,
        g_b_ada,
        g_w_qkv,
        g_w_out,
        g_w_up,
        g_b_up,
        g_w_down,
        g_b_down,
    )


def solution(mesh):
    shards = ("dp", "seq")
    placed = (
        (P("dp", "seq", None), P("dp", None), P("dp"))
        + (P(),) * 10
        + (P("dp", "seq", None),)
    )
    return jax.shard_map(
        functools.partial(body, mesh.shape["dp"], mesh.shape["seq"]),
        mesh=mesh,
        in_specs=placed,
        out_specs=(
            P("dp", "seq", None),
            P("dp", "seq", None),
            P("dp", None),
            P(shards),
            P(shards),
            P(None, shards),
            P(shards),
            P(shards, None),
            P(shards, None),
            P(shards, None),
            P(shards),
            P(shards, None),
            P(shards),
        ),
        check_vma=False,
    )
```

time: 1440 us -> 512 us (0.36)
  waiting for transfers between devices: 971 us -> 118 us
  matrix products: 237 us -> 41.1 us
  starting transfers between devices: 1.42 us -> 108 us
  Pallas kernels: 0 us -> 97.7 us
  blocking collectives: 53.9 us -> 0 us
  other arithmetic: 98 us -> 58.5 us
  local copies, waits for them, and re-layouts: 58.7 us -> 83.8 us
    reduce_scatter x7 -> x0, waiting for transfers between devices: 660 us -> none  [the longest x1 142 us: body(): lax.psum_scatter(grad_w_down, ('dp', 'seq'), scatter_dimension=0, tiled=T...]
    all_gather x4 -> x0, waiting for transfers between devices: 311 us -> none  [the longest x2 171 us: body(): lax.all_gather(early_part[6], 'seq', axis=1, tiled=True)]
    dot_general x45 -> x21, matrix products: 237 us -> 41.1 us  [the longest x9 25.2 us: nt(): lax.dot_general(left, right, (((1,), (1,)), ((), ())), preferred_element_...]
    ppermute x0 -> x54, waiting for transfers between devices: none -> 118 us  [the longest x18 79.6 us: seq_swap(): return lax.ppermute(value, 'seq', [(i, i ^ bit) for i in range(seq_size)])]
    ppermute x0 -> x54, starting transfers between devices: none -> 108 us  [the longest x26 55 us: dp_swap(): lax.ppermute(value, 'dp', [(i, i ^ 1 << bit) for i in range(dp_size)])]
    pallas_call x0 -> x10, Pallas kernels: none -> 97.7 us  [the longest x1 44.2 us: feed_forward(): pl.pallas_call(mlp_kernel, grid=(2 * tiles,), in_specs=[whole(m) for m in...]
    unnamed x1 -> x0, blocking collectives: 42.6 us -> none
    sub x4 -> x0, other arithmetic: 20.6 us -> none  [the longest x3 19.8 us: single(): raised = jnp.exp(scores - row_max)]
  transfers between devices with their start and end apart: 11 -> 54, of which waited for: 11 -> 18; matrix products, arithmetic and copies ran while one was open for 8% -> 32% of each run, Pallas kernels for 0% -> 9%
where the time goes in v1:
time: 512 us; the launch traced here: 510 us
  waiting for transfers between devices  118 us (23%)
  starting transfers between devices  108 us (21%)
  Pallas kernels  97.7 us (19%)
  local copies, waits for them, and re-layouts  83.8 us (16%)
  other arithmetic  58.5 us (11%)
  matrix products  41.1 us (8%)
    ppermute x18, waiting for transfers between devices, seq_swap(): return lax.ppermute(value, 'seq', [(i, i ^ bit) for i in range(seq_size)])  79.6 us
    ppermute x26, starting transfers between devices, dp_swap(): lax.ppermute(value, 'dp', [(i, i ^ 1 << bit) for i in range(dp_size)])  55 us
    pallas_call x1, Pallas kernels, feed_forward(): pl.pallas_call(mlp_kernel, grid=(2 * tiles,), in_specs=[whole(m) for m in...  44.2 us
    ppermute x18, starting transfers between devices, seq_swap(): return lax.ppermute(value, 'seq', [(i, i ^ bit) for i in range(seq_size)])  40.4 us
    ppermute x26, waiting for transfers between devices, dp_swap(): lax.ppermute(value, 'dp', [(i, i ^ 1 << bit) for i in range(dp_size)])  38.6 us
    pallas_call x3, Pallas kernels, attend_back(): pl.pallas_call(attend_back_kernel, grid_spec=pltpu.PrefetchScalarGridSpec...  25.5 us
    dot_general x9, matrix products, nt(): lax.dot_general(left, right, (((1,), (1,)), ((), ())), preferred_element_...  25.2 us
    add x25, other arithmetic, reduce_rows(): held = keep + got.astype(F32)  19.8 us
  transfers between devices with their start and end apart: 54, of which 18 were waited for; matrix products, arithmetic and copies ran while one was open for 32% of the time, Pallas kernels for 9%

profile of v1, /device:TPU:0, one launch (start us, length us, event | category | flops | bytes accessed | tf_op | source)
XLA Modules:
  0.0 510.4 jit_solution(16661892623974573999)
XLA Ops:
  7.2 8.4 %collective-permute-start = (s32[3]{0:T(128)}, s32[3]{0:T(128)}, u32[]{:S(2)}, u32[]{:S(2)}) collective-permute-start(s32[3]{0:T(128)} %param.17), channel_id=1, source_target_pairs={{0,4},{4,0},{8,12},{12,8},{16,20},{20,16},{24,28},{28,24},{1,5},{5... | collective-permute-start | bytes 44 | tf_op jit(solution)/shard_map/ppermute | solution.py:438
  51.0 31.1 %collective-permute-done.9 = bf16[256,768]{1,0:T(8,128)(2,1)S(1)} collective-permute-done((bf16[256,768]{1,0:T(8,128)(2,1)S(1)}, bf16[256,768]{1,0:T(8,128)(2,1)S(1)}, u32[]{:S(2)}, u32[]{:S(2)}) %collective-permute-start.9) | collective-permute-done | bytes 393248 | tf_op jit(solution)/shard_map/ppermute | solution.py:441
  88.5 4.7 shard_map.250
  97.0 5.2 %shard_map.251 = (bf16[256,768]{1,0:T(8,128)(2,1)S(1)}, f32[3,8,256]{2,1,0:T(8,128)S(1)}) custom-call(s32[2]{0:T(128)S(1)} %pad_add_fusion.2.place, bf16[256,768]{1,0:T(8,128)(2,1)S(1)} %get-tuple-element.56.q_ref, bf16[1024,768]{1,0:T(8,128)(2,1)S(1)} %get-tuple-element.57.k_ref, bf16[1024,768]{1,0:T(8,128)(2,1)S(1)} %get-tuple-element.58.v_ref), custom_call_target="tpu_custom_call" | custom-call | flops 3221225472 | bytes 5000000 | tf_op jit(solution)/shard_map/pallas_call | solution.py:307
  103.0 4.3 shard_map.249
  107.3 4.9 shard_map.246
  112.3 5.2 %shard_map.247 = (bf16[256,768]{1,0:T(8,128)(2,1)S(1)}, f32[3,8,256]{2,1,0:T(8,128)S(1)}) custom-call(s32[2]{0:T(128)S(1)} %pad_add_fusion.place, bf16[256,768]{1,0:T(8,128)(2,1)S(1)} %get-tuple-element.48.q_ref, bf16[1024,768]{1,0:T(8,128)(2,1)S(1)} %get-tuple-element.49.k_ref, bf16[1024,768]{1,0:T(8,128)(2,1)S(1)} %get-tuple-element.50.v_ref), custom_call_target="tpu_custom_call" | custom-call | flops 3221225472 | bytes 5000000 | tf_op jit(solution)/shard_map/pallas_call | solution.py:307
  118.3 44.2 %shard_map.252 = (bf16[3,256,768]{2,1,0:T(8,128)(2,1)}, f32[3,256,768]{2,1,0:T(8,128)}, bf16[3,256,768]{2,1,0:T(8,128)(2,1)}, f32[768,768]{1,0:T(8,128)}, f32[24...) custom-call(bf16[256,768]{1,0:T(8,128)(2,1)} %copy-done.35, ...), custom_call_target="tpu_custom_call" | custom-call | flops 24461180928 | bytes 50000000 | tf_op jit(solution)/shard_map/pallas_call | solution.py:375
  162.5 4.0 fusion.1
  167.0 4.2 fusion
  173.8 9.3 %shard_map.253 = (bf16[256,768]{1,0:T(8,128)(2,1)S(1)}, bf16[1024,768]{1,0:T(8,128)(2,1)S(1)}, bf16[1024,768]{1,0:T(8,128)(2,1)S(1)}) custom-call(s32[2]{0:T(128)S(1)} %pad_add_fusion.place, bf16[256,768]{1,0:T(8,128)(2,1)S(1)} %copy-done.32, bf16[1024,768]{1,0:T(8,128)(2,1)} %copy-done.25, bf16[1024,768]{1,0:T(8,128)(2,1)} %copy-done.26, ...), custom_call_target="tpu_custom_call" | custom-call | flops 8053063680 | bytes 9000000 | tf_op jit(solution)/shard_map/pallas_call | solution.py:332
  183.1 5.1 fusion.129
  191.1 6.5 %shard_map.254 = (bf16[256,768]{1,0:T(8,128)(2,1)S(1)}, bf16[1024,768]{1,0:T(8,128)(2,1)S(1)}, bf16[1024,768]{1,0:T(8,128)(2,1)S(1)}) custom-call(s32[2]{0:T(128)S(1)} %pad_add_fusion.1.place, bf16[256,768]{1,0:T(8,128)(2,1)S(1)} %copy-done.30, bf16[1024,768]{1,0:T(8,128)(2,1)} %copy-done.23, bf16[1024,768]{1,0:T(8,128)(2,1)} %copy-done.24, ...), custom_call_target="tpu_custom_call" | custom-call | flops 8053063680 | bytes 9000000 | tf_op jit(solution)/shard_map/pallas_call | solution.py:332
  198.7 4.5 fusion.127
  206.2 9.8 %shard_map.255 = (bf16[256,768]{1,0:T(8,128)(2,1)S(1)}, bf16[1024,768]{1,0:T(8,128)(2,1)S(1)}, bf16[1024,768]{1,0:T(8,128)(2,1)S(1)}) custom-call(s32[2]{0:T(128)S(1)} %pad_add_fusion.2.place, bf16[256,768]{1,0:T(8,128)(2,1)S(1)} %copy-done.28, bf16[1024,768]{1,0:T(8,128)(2,1)} %copy-done.21, bf16[1024,768]{1,0:T(8,128)(2,1)} %copy-done.22, ...), custom_call_target="tpu_custom_call" | custom-call | flops 8053063680 | bytes 9000000 | tf_op jit(solution)/shard_map/pallas_call | solution.py:332
  220.1 4.5 fusion.125
  231.9 5.2 %copy.297 = f32[768,1152]{1,0:T(8,128)} copy(f32[768,1152]{0,1:T(8,128)} %get-tuple-element.131) | data formatting | bytes 7077888 | tf_op jit(solution)/shard_map/slice | solution.py:544
  239.6 5.5 %copy.295 = f32[768,1152]{1,0:T(8,128)} copy(f32[768,1152]{0,1:T(8,128)} %get-tuple-element.130) | data formatting | bytes 7077888 | tf_op jit(solution)/shard_map/slice | solution.py:543
  267.8 28.8 %collective-permute-start.40 = (bf16[2,2,2,24,768]{4,3,1,2,0:T(8,128)(2,1)S(1)}, bf16[2,2,2,24,768]{4,3,1,2,0:T(8,128)(2,1)S(1)}, u32[]{:S(2)}, u32[]{:S(2)}) collective-permute-start(bf16[2,2,2,24,768]{4,3,1,2,0:T(8,128)(2,1)S(1)} %fusion.76), channel_id=1, source_target_pairs={{0,16},{4,20},{8,24},{12,28},{16,0},{20,4},{24,8},{28,12},{1,17},{... | collective-permute-start | bytes 884744 | tf_op jit(solution)/shard_map/ppermute | solution.py:438
  299.8 4.3 collective-permute-done.40
  314.7 5.3 %collective-permute-done.42 = bf16[2,24,768]{2,1,0:T(8,128)(2,1)S(1)} collective-permute-done((bf16[2,24,768]{2,1,0:T(8,128)(2,1)S(1)}, bf16[2,24,768]{2,1,0:T(8,128)(2,1)S(1)}, u32[]{:S(2)}, u32[]{:S(2)}) %collective-permute-start.42) | collective-permute-done | bytes 73760 | tf_op jit(solution)/shard_map/ppermute | solution.py:441
  320.1 9.4 %collective-permute-start.43 = (bf16[24,768]{1,0:T(8,128)(2,1)S(1)}, bf16[24,768]{1,0:T(8,128)(2,1)S(1)}, u32[]{:S(2)}, u32[]{:S(2)}) collective-permute-start(bf16[24,768]{1,0:T(8,128)(2,1)S(1)} %fusion.89), channel_id=1, source_target_pairs={{0,2},{1,3},{2,0},{3,1},{4,6},{5,7},{6,4},{7,5},{8,10},{9,11},{10,... | collective-permute-start | bytes 110600 | tf_op jit(solution)/shard_map/ppermute | solution.py:441
  330.3 6.4 %collective-permute-done.43 = bf16[24,768]{1,0:T(8,128)(2,1)S(1)} collective-permute-done((bf16[24,768]{1,0:T(8,128)(2,1)S(1)}, bf16[24,768]{1,0:T(8,128)(2,1)S(1)}, u32[]{:S(2)}, u32[]{:S(2)}) %collective-permute-start.43) | collective-permute-done | bytes 36896 | tf_op jit(solution)/shard_map/ppermute | solution.py:441
  340.0 8.7 %collective-permute-done.19 = bf16[256,768]{1,0:T(8,128)(2,1)S(1)} collective-permute-done((bf16[256,768]{1,0:T(8,128)(2,1)S(1)}, bf16[256,768]{1,0:T(8,128)(2,1)S(1)}, u32[]{:S(2)}, u32[]{:S(2)}) %collective-permute-start.19) | collective-permute-done | bytes 393248 | tf_op jit(solution)/shard_map/ppermute | solution.py:441
  403.2 5.7 %collective-permute-done.31 = bf16[2,2,24,1152]{3,2,1,0:T(8,128)(2,1)S(1)} collective-permute-done((bf16[2,2,24,1152]{3,2,1,0:T(8,128)(2,1)S(1)}, bf16[2,2,24,1152]{3,2,1,0:T(8,128)(2,1)S(1)}, u32[]{:S(2)}, u32[]{:S(2)}) %collective-permute-start.31) | collective-permute-done | bytes 221216 | tf_op jit(solution)/shard_map/ppermute | solution.py:438
  415.0 11.4 %collective-permute-start.38 = (bf16[24,1152]{1,0:T(8,128)(2,1)S(1)}, bf16[24,1152]{1,0:T(8,128)(2,1)S(1)}, u32[]{:S(2)}, u32[]{:S(2)}) collective-permute-start(bf16[24,1152]{1,0:T(8,128)(2,1)S(1)} %fusion.88), channel_id=1, source_target_pairs={{0,2},{1,3},{2,0},{3,1},{4,6},{5,7},{6,4},{7,5},{8,10},{9,11},{10,... | collective-permute-start | bytes 165896 | tf_op jit(solution)/shard_map/ppermute | solution.py:441
  426.6 5.8 %bitcast_add_fusion = f32[2,2,2,2,96,768]{5,4,2,3,1,0:T(8,128)} fusion(bf16[2,2,2,2,96,768]{5,4,2,3,1,0:T(8,128)(2,1)} %collective-permute-done.49, f32[2,2,2,2,2,96,768]{6,5,4,3,2,1,0:T(8,128)} %bitcast.326, s32[]{:T(128)S(6)} %select_n.250), kind=kLoop, calls=%fused_computation.3 | loop fusion | flops 2359296 | bytes 11796484 | tf_op jit(solution)/shard_map/add | solution.py:502
  454.1 7.4 %collective-permute-done.50 = bf16[2,2,2,96,768]{4,3,1,2,0:T(8,128)(2,1)} collective-permute-done((bf16[2,2,2,96,768]{4,3,1,2,0:T(8,128)(2,1)S(1)}, bf16[2,2,2,96,768]{4,3,1,2,0:T(8,128)(2,1)}, u32[]{:S(2)}, u32[]{:S(2)}) %collective-permute-start.50) | collective-permute-done | bytes 1179680 | tf_op jit(solution)/shard_map/ppermute | solution.py:438
  471.4 9.8 %collective-permute-done.51 = bf16[2,2,96,768]{3,2,0,1:T(8,128)(2,1)S(1)} collective-permute-done((bf16[2,2,96,768]{3,2,0,1:T(8,128)(2,1)S(1)}, bf16[2,2,96,768]{3,2,0,1:T(8,128)(2,1)S(1)}, u32[]{:S(2)}, u32[]{:S(2)}) %collective-permute-start.51) | collective-permute-done | bytes 589856 | tf_op jit(solution)/shard_map/ppermute | solution.py:438
  487.2 5.5 %collective-permute-done.52 = bf16[2,96,768]{2,1,0:T(8,128)(2,1)S(1)} collective-permute-done((bf16[2,96,768]{2,1,0:T(8,128)(2,1)S(1)}, bf16[2,96,768]{2,1,0:T(8,128)(2,1)S(1)}, u32[]{:S(2)}, u32[]{:S(2)}) %collective-permute-start.52) | collective-permute-done | bytes 294944 | tf_op jit(solution)/shard_map/ppermute | solution.py:441
  494.6 6.7 %collective-permute-done.47 = bf16[2,24,3072]{2,1,0:T(8,128)(2,1)S(1)} collective-permute-done((bf16[2,24,3072]{2,1,0:T(8,128)(2,1)S(1)}, bf16[2,24,3072]{2,1,0:T(8,128)(2,1)S(1)}, u32[]{:S(2)}, u32[]{:S(2)}) %collective-permute-start.47) | collective-permute-done | bytes 294944 | tf_op jit(solution)/shard_map/ppermute | solution.py:441
  502.2 7.2 %collective-permute-done.48 = bf16[24,3072]{1,0:T(8,128)(2,1)S(1)} collective-permute-done((bf16[24,3072]{1,0:T(8,128)(2,1)S(1)}, bf16[24,3072]{1,0:T(8,128)(2,1)S(1)}, u32[]{:S(2)}, u32[]{:S(2)}) %collective-permute-start.48) | collective-permute-done | bytes 147488 | tf_op jit(solution)/shard_map/ppermute | solution.py:441
  (573 shorter events, 218.2 us)
Async XLA Ops:
  3.0 40.0 %collective-permute-start.1 = (bf16[256,768]{1,0:T(8,128)(2,1)}, bf16[256,768]{1,0:T(8,128)(2,1)}, u32[]{:S(2)}, u32[]{:S(2)}) collective-permute-start(bf16[256,768]{1,0:T(8,128)(2,1)} %get-tuple-element.143), channel_id=1, source_target_pairs={{2,4},{3,5},{4,2},{5,3},{10,12},{11,13},{12,10},{13,11},{18,20},{1... | collective-permute-start | bytes 1179656 | tf_op jit(solution)/shard_map/ppermute | solution.py:450
  4.5 39.4 %collective-permute-start.5 = (bf16[256,768]{1,0:T(8,128)(2,1)}, bf16[256,768]{1,0:T(8,128)(2,1)}, u32[]{:S(2)}, u32[]{:S(2)}) collective-permute-start(bf16[256,768]{1,0:T(8,128)(2,1)} %get-tuple-element.144), channel_id=1, source_target_pairs={{2,4},{3,5},{4,2},{5,3},{10,12},{11,13},{12,10},{13,11},{18,20},{1... | collective-permute-start | bytes 1179656 | tf_op jit(solution)/shard_map/ppermute | solution.py:450
  5.9 38.1 %collective-permute-start.8 = (bf16[256,768]{1,0:T(8,128)(2,1)}, bf16[256,768]{1,0:T(8,128)(2,1)}, u32[]{:S(2)}, u32[]{:S(2)}) collective-permute-start(bf16[256,768]{1,0:T(8,128)(2,1)} %get-tuple-element.142), channel_id=1, source_target_pairs={{2,4},{3,5},{4,2},{5,3},{10,12},{11,13},{12,10},{13,11},{18,20},{1... | collective-permute-start | bytes 1179656 | tf_op jit(solution)/shard_map/ppermute | solution.py:450
  7.2 27.4 %collective-permute-start = (s32[3]{0:T(128)}, s32[3]{0:T(128)}, u32[]{:S(2)}, u32[]{:S(2)}) collective-permute-start(s32[3]{0:T(128)} %param.17), channel_id=1, source_target_pairs={{0,4},{4,0},{8,12},{12,8},{16,20},{20,16},{24,28},{28,24},{1,5},{5... | collective-permute-start | bytes 44 | tf_op jit(solution)/shard_map/ppermute | solution.py:438
  15.7 23.9 %collective-permute-start.4 = (bf16[3,128]{1,0:T(4,128)(2,1)S(1)}, bf16[3,128]{1,0:T(4,128)(2,1)S(1)}, u32[]{:S(2)}, u32[]{:S(2)}) collective-permute-start(bf16[3,128]{1,0:T(4,128)(2,1)S(1)} %copy-done.117), channel_id=1, source_target_pairs={{0,4},{4,0},{8,12},{12,8},{16,20},{20,16},{24,28},{28,24},{1,5},{5... | collective-permute-start | bytes 2312 | tf_op jit(solution)/shard_map/ppermute | solution.py:438
  45.6 40.0 %collective-permute-start.6 = (bf16[256,768]{1,0:T(8,128)(2,1)S(1)}, bf16[256,768]{1,0:T(8,128)(2,1)S(1)}, u32[]{:S(2)}, u32[]{:S(2)}) collective-permute-start(bf16[256,768]{1,0:T(8,128)(2,1)S(1)} %get-tuple-element.139), channel_id=1, source_target_pairs={{0,1},{1,0},{2,3},{3,2},{4,5},{5,4},{6,7},{7,6},{8,9},{9,8},{10,11... | collective-permute-start | bytes 1179656 | tf_op jit(solution)/shard_map/ppermute | solution.py:441
  47.3 40.6 %collective-permute-start.2 = (bf16[256,768]{1,0:T(8,128)(2,1)S(1)}, bf16[256,768]{1,0:T(8,128)(2,1)S(1)}, u32[]{:S(2)}, u32[]{:S(2)}) collective-permute-start(bf16[256,768]{1,0:T(8,128)(2,1)S(1)} %get-tuple-element.141), channel_id=1, source_target_pairs={{0,1},{1,0},{2,3},{3,2},{4,5},{5,4},{6,7},{7,6},{8,9},{9,8},{10,11... | collective-permute-start | bytes 1179656 | tf_op jit(solution)/shard_map/ppermute | solution.py:441
  48.7 33.5 %collective-permute-start.9 = (bf16[256,768]{1,0:T(8,128)(2,1)S(1)}, bf16[256,768]{1,0:T(8,128)(2,1)S(1)}, u32[]{:S(2)}, u32[]{:S(2)}) collective-permute-start(bf16[256,768]{1,0:T(8,128)(2,1)S(1)} %get-tuple-element.118), channel_id=1, source_target_pairs={{0,1},{1,0},{2,3},{3,2},{4,5},{5,4},{6,7},{7,6},{8,9},{9,8},{10,11... | collective-permute-start | bytes 1179656 | tf_op jit(solution)/shard_map/ppermute | solution.py:441
  87.9 19.4 %collective-permute-start.3 = (bf16[2,256,768]{2,1,0:T(8,128)(2,1)S(1)}, bf16[2,256,768]{2,1,0:T(8,128)(2,1)S(1)}, u32[]{:S(2)}, u32[]{:S(2)}) collective-permute-start(bf16[2,256,768]{2,1,0:T(8,128)(2,1)S(1)} %pad_maximum_fusion.5.near_ref), channel_id=1, source_target_pairs={{0,4},{4,0},{8,12},{12,8},{16,20},{20,16},{24,28},{28,24},{1,5},{5... | collective-permute-start | bytes 2359304 | tf_op jit(solution)/shard_map/ppermute | solution.py:438
  166.5 260.1 %collective-permute-start.49 = (bf16[2,2,2,2,96,768]{5,4,2,3,1,0:T(8,128)(2,1)}, bf16[2,2,2,2,96,768]{5,4,2,3,1,0:T(8,128)(2,1)}, u32[]{:S(2)}, u32[]{:S(2)}) collective-permute-start(bf16[2,2,2,2,96,768]{5,4,2,3,1,0:T(8,128)(2,1)} %fusion.1), channel_id=1, source_target_pairs={{0,4},{4,0},{8,12},{12,8},{16,20},{20,16},{24,28},{28,24},{1,5},{5... | collective-permute-start | bytes 7077896 | tf_op jit(solution)/shard_map/ppermute | solution.py:438
  171.2 264.9 %collective-permute-start.44 = (bf16[2,2,2,2,24,3072]{5,4,2,3,0,1:T(8,128)(2,1)}, bf16[2,2,2,2,24,3072]{5,4,2,3,0,1:T(8,128)(2,1)}, u32[]{:S(2)}, u32[]{:S(2)}) collective-permute-start(bf16[2,2,2,2,24,3072]{5,4,2,3,0,1:T(8,128)(2,1)} %fusion), channel_id=1, source_target_pairs={{0,4},{4,0},{8,12},{12,8},{16,20},{20,16},{24,28},{28,24},{1,5},{5... | collective-permute-start | bytes 7077896 | tf_op jit(solution)/shard_map/ppermute | solution.py:438
  173.4 90.6 %collective-permute-start.39 = (bf16[2,2,2,2,24,768]{5,4,2,3,1,0:T(8,128)(2,1)}, bf16[2,2,2,2,24,768]{5,4,2,3,1,0:T(8,128)(2,1)}, u32[]{:S(2)}, u32[]{:S(2)}) collective-permute-start(bf16[2,2,2,2,24,768]{5,4,2,3,1,0:T(8,128)(2,1)} %fusion.62), channel_id=1, source_target_pairs={{0,4},{4,0},{8,12},{12,8},{16,20},{20,16},{24,28},{28,24},{1,5},{5... | collective-permute-start | bytes 1769480 | tf_op jit(solution)/shard_map/ppermute | solution.py:438
  250.9 15.4 %collective-permute-start.15 = (bf16[2,256,768]{2,1,0:T(8,128)(2,1)}, bf16[2,256,768]{2,1,0:T(8,128)(2,1)}, u32[]{:S(2)}, u32[]{:S(2)}) collective-permute-start(bf16[2,256,768]{2,1,0:T(8,128)(2,1)} %pad_maximum_fusion.8), channel_id=1, source_target_pairs={{0,4},{4,0},{8,12},{12,8},{16,20},{20,16},{24,28},{28,24},{1,5},{5... | collective-permute-start | bytes 2359304 | tf_op jit(solution)/shard_map/ppermute | solution.py:438
  264.0 34.0 %collective-permute-start.18 = (bf16[2,256,768]{2,1,0:T(8,128)(2,1)S(1)}, bf16[2,256,768]{2,1,0:T(8,128)(2,1)S(1)}, u32[]{:S(2)}, u32[]{:S(2)}) collective-permute-start(bf16[2,256,768]{2,1,0:T(8,128)(2,1)S(1)} %pad_maximum_fusion.9), channel_id=1, source_target_pairs={{0,4},{4,0},{8,12},{12,8},{16,20},{20,16},{24,28},{28,24},{1,5},{5... | collective-permute-start | bytes 2359304 | tf_op jit(solution)/shard_map/ppermute | solution.py:438
  266.3 39.6 %collective-permute-start.34 = (bf16[2,2,2,2,24,1152]{5,4,2,3,1,0:T(8,128)(2,1)S(1)}, bf16[2,2,2,2,24,1152]{5,4,2,3,1,0:T(8,128)(2,1)S(1)}, u32[]{:S(2)}, u32[]{:S(2)}) collective-permute-start(bf16[2,2,2,2,24,1152]{5,4,2,3,1,0:T(8,128)(2,1)S(1)} %copy-done.71), channel_id=1, source_target_pairs={{0,4},{4,0},{8,12},{12,8},{16,20},{20,16},{24,28},{28,24},{1,5},{5... | collective-permute-start | bytes 2654216 | tf_op jit(solution)/shard_map/ppermute | solution.py:438
  267.8 36.3 %collective-permute-start.40 = (bf16[2,2,2,24,768]{4,3,1,2,0:T(8,128)(2,1)S(1)}, bf16[2,2,2,24,768]{4,3,1,2,0:T(8,128)(2,1)S(1)}, u32[]{:S(2)}, u32[]{:S(2)}) collective-permute-start(bf16[2,2,2,24,768]{4,3,1,2,0:T(8,128)(2,1)S(1)} %fusion.76), channel_id=1, source_target_pairs={{0,16},{4,20},{8,24},{12,28},{16,0},{20,4},{24,8},{28,12},{1,17},{... | collective-permute-start | bytes 884744 | tf_op jit(solution)/shard_map/ppermute | solution.py:438
  304.1 61.5 %collective-permute-start.14 = (bf16[3,256,768]{2,1,0:T(8,128)(2,1)}, bf16[3,256,768]{2,1,0:T(8,128)(2,1)}, u32[]{:S(2)}, u32[]{:S(2)}) collective-permute-start(bf16[3,256,768]{2,1,0:T(8,128)(2,1)} %get-tuple-element.60), channel_id=1, source_target_pairs={{2,4},{3,5},{4,2},{5,3},{10,12},{11,13},{12,10},{13,11},{18,20},{1... | collective-permute-start | bytes 3538952 | tf_op jit(solution)/shard_map/ppermute | solution.py:450
  305.9 31.5 %collective-permute-start.22 = (bf16[256,768]{1,0:T(8,128)(2,1)S(1)}, bf16[256,768]{1,0:T(8,128)(2,1)S(1)}, u32[]{:S(2)}, u32[]{:S(2)}) collective-permute-start(bf16[256,768]{1,0:T(8,128)(2,1)S(1)} %fusion.67), channel_id=1, source_target_pairs={{0,1},{1,0},{2,3},{3,2},{4,5},{5,4},{6,7},{7,6},{8,9},{9,8},{10,11... | collective-permute-start | bytes 1179656 | tf_op jit(solution)/shard_map/ppermute | solution.py:441
  320.1 16.7 %collective-permute-start.43 = (bf16[24,768]{1,0:T(8,128)(2,1)S(1)}, bf16[24,768]{1,0:T(8,128)(2,1)S(1)}, u32[]{:S(2)}, u32[]{:S(2)}) collective-permute-start(bf16[24,768]{1,0:T(8,128)(2,1)S(1)} %fusion.89), channel_id=1, source_target_pairs={{0,2},{1,3},{2,0},{3,1},{4,6},{5,7},{6,4},{7,5},{8,10},{9,11},{10,... | collective-permute-start | bytes 110600 | tf_op jit(solution)/shard_map/ppermute | solution.py:441
  337.4 16.2 %collective-permute-start.16 = (bf16[256,768]{1,0:T(8,128)(2,1)S(1)}, bf16[256,768]{1,0:T(8,128)(2,1)S(1)}, u32[]{:S(2)}, u32[]{:S(2)}) collective-permute-start(bf16[256,768]{1,0:T(8,128)(2,1)S(1)} %fusion.65), channel_id=1, source_target_pairs={{0,1},{1,0},{2,3},{3,2},{4,5},{5,4},{6,7},{7,6},{8,9},{9,8},{10,11... | collective-permute-start | bytes 1179656 | tf_op jit(solution)/shard_map/ppermute | solution.py:441
  348.8 44.7 %collective-permute-start.35 = (bf16[2,2,2,24,1152]{4,3,1,2,0:T(8,128)(2,1)}, bf16[2,2,2,24,1152]{4,3,1,2,0:T(8,128)(2,1)}, u32[]{:S(2)}, u32[]{:S(2)}) collective-permute-start(bf16[2,2,2,24,1152]{4,3,1,2,0:T(8,128)(2,1)} %fusion.64), channel_id=1, source_target_pairs={{0,16},{4,20},{8,24},{12,28},{16,0},{20,4},{24,8},{28,12},{1,17},{... | collective-permute-start | bytes 1327112 | tf_op jit(solution)/shard_map/ppermute | solution.py:438
  353.5 42.0 %collective-permute-start.30 = (bf16[2,2,2,24,1152]{4,3,2,1,0:T(8,128)(2,1)}, bf16[2,2,2,24,1152]{4,3,2,1,0:T(8,128)(2,1)}, u32[]{:S(2)}, u32[]{:S(2)}) collective-permute-start(bf16[2,2,2,24,1152]{4,3,2,1,0:T(8,128)(2,1)} %fusion.63), channel_id=1, source_target_pairs={{0,8},{4,12},{8,0},{12,4},{16,24},{20,28},{24,16},{28,20},{1,9},{5... | collective-permute-start | bytes 1327112 | tf_op jit(solution)/shard_map/ppermute | solution.py:438
  389.1 20.8 %collective-permute-start.17 = (bf16[256,768]{1,0:T(8,128)(2,1)}, bf16[256,768]{1,0:T(8,128)(2,1)}, u32[]{:S(2)}, u32[]{:S(2)}) collective-permute-start(bf16[256,768]{1,0:T(8,128)(2,1)} %get-tuple-element.107), channel_id=1, source_target_pairs={{2,4},{3,5},{4,2},{5,3},{10,12},{11,13},{12,10},{13,11},{18,20},{1... | collective-permute-start | bytes 1179656 | tf_op jit(solution)/shard_map/ppermute | solution.py:538
  393.4 18.3 %collective-permute-start.20 = (bf16[256,768]{1,0:T(8,128)(2,1)}, bf16[256,768]{1,0:T(8,128)(2,1)S(1)}, u32[]{:S(2)}, u32[]{:S(2)}) collective-permute-start(bf16[256,768]{1,0:T(8,128)(2,1)} %get-tuple-element.128), channel_id=1, source_target_pairs={{2,4},{3,5},{4,2},{5,3},{10,12},{11,13},{12,10},{13,11},{18,20},{1... | collective-permute-start | bytes 1179656 | tf_op jit(solution)/shard_map/ppermute | solution.py:538
  411.8 14.7 %collective-permute-start.32 = (bf16[2,24,1152]{2,1,0:T(8,128)(2,1)S(1)}, bf16[2,24,1152]{2,1,0:T(8,128)(2,1)S(1)}, u32[]{:S(2)}, u32[]{:S(2)}) collective-permute-start(bf16[2,24,1152]{2,1,0:T(8,128)(2,1)S(1)} %fusion.84), channel_id=1, source_target_pairs={{0,1},{1,0},{2,3},{3,2},{4,5},{5,4},{6,7},{7,6},{8,9},{9,8},{10,11... | collective-permute-start | bytes 331784 | tf_op jit(solution)/shard_map/ppermute | solution.py:441
  415.0 27.4 %collective-permute-start.38 = (bf16[24,1152]{1,0:T(8,128)(2,1)S(1)}, bf16[24,1152]{1,0:T(8,128)(2,1)S(1)}, u32[]{:S(2)}, u32[]{:S(2)}) collective-permute-start(bf16[24,1152]{1,0:T(8,128)(2,1)S(1)} %fusion.88), channel_id=1, source_target_pairs={{0,2},{1,3},{2,0},{3,1},{4,6},{5,7},{6,4},{7,5},{8,10},{9,11},{10,... | collective-permute-start | bytes 165896 | tf_op jit(solution)/shard_map/ppermute | solution.py:441
  426.5 15.9 %collective-permute-start.33 = (bf16[24,1152]{1,0:T(8,128)(2,1)S(1)}, bf16[24,1152]{1,0:T(8,128)(2,1)S(1)}, u32[]{:S(2)}, u32[]{:S(2)}) collective-permute-start(bf16[24,1152]{1,0:T(8,128)(2,1)S(1)} %fusion.87), channel_id=1, source_target_pairs={{0,2},{1,3},{2,0},{3,1},{4,6},{5,7},{6,4},{7,5},{8,10},{9,11},{10,... | collective-permute-start | bytes 165896 | tf_op jit(solution)/shard_map/ppermute | solution.py:441
  434.2 27.4 %collective-permute-start.50 = (bf16[2,2,2,96,768]{4,3,1,2,0:T(8,128)(2,1)S(1)}, bf16[2,2,2,96,768]{4,3,1,2,0:T(8,128)(2,1)}, u32[]{:S(2)}, u32[]{:S(2)}) collective-permute-start(bf16[2,2,2,96,768]{4,3,1,2,0:T(8,128)(2,1)S(1)} %fusion.9), channel_id=1, source_target_pairs={{0,16},{4,20},{8,24},{12,28},{16,0},{20,4},{24,8},{28,12},{1,17},{... | collective-permute-start | bytes 3538952 | tf_op jit(solution)/shard_map/ppermute | solution.py:438
  441.0 27.7 %collective-permute-start.45 = (bf16[2,2,2,24,3072]{4,3,1,2,0:T(8,128)(2,1)S(1)}, bf16[2,2,2,24,3072]{4,3,1,2,0:T(8,128)(2,1)}, u32[]{:S(2)}, u32[]{:S(2)}) collective-permute-start(bf16[2,2,2,24,3072]{4,3,1,2,0:T(8,128)(2,1)S(1)} %fusion.8), channel_id=1, source_target_pairs={{0,8},{4,12},{8,0},{12,4},{16,24},{20,28},{24,16},{28,20},{1,9},{5... | collective-permute-start | bytes 3538952 | tf_op jit(solution)/shard_map/ppermute | solution.py:438
  464.1 17.1 %collective-permute-start.51 = (bf16[2,2,96,768]{3,2,0,1:T(8,128)(2,1)S(1)}, bf16[2,2,96,768]{3,2,0,1:T(8,128)(2,1)S(1)}, u32[]{:S(2)}, u32[]{:S(2)}) collective-permute-start(bf16[2,2,96,768]{3,2,0,1:T(8,128)(2,1)S(1)} %fusion.61), channel_id=1, source_target_pairs={{0,8},{4,12},{8,0},{12,4},{16,24},{20,28},{24,16},{28,20},{1,9},{5... | collective-permute-start | bytes 1769480 | tf_op jit(solution)/shard_map/ppermute | solution.py:438
  470.4 14.5 %collective-permute-start.46 = (bf16[2,2,24,3072]{3,2,0,1:T(8,128)(2,1)S(1)}, bf16[2,2,24,3072]{3,2,0,1:T(8,128)(2,1)S(1)}, u32[]{:S(2)}, u32[]{:S(2)}) collective-permute-start(bf16[2,2,24,3072]{3,2,0,1:T(8,128)(2,1)S(1)} %fusion.60), channel_id=1, source_target_pairs={{0,16},{4,20},{8,24},{12,28},{16,0},{20,4},{24,8},{28,12},{1,17},{... | collective-permute-start | bytes 1769480 | tf_op jit(solution)/shard_map/ppermute | solution.py:438
  485.1 16.2 %collective-permute-start.47 = (bf16[2,24,3072]{2,1,0:T(8,128)(2,1)S(1)}, bf16[2,24,3072]{2,1,0:T(8,128)(2,1)S(1)}, u32[]{:S(2)}, u32[]{:S(2)}) collective-permute-start(bf16[2,24,3072]{2,1,0:T(8,128)(2,1)S(1)} %fusion.77), channel_id=1, source_target_pairs={{0,1},{1,0},{2,3},{3,2},{4,5},{5,4},{6,7},{7,6},{8,9},{9,8},{10,11... | collective-permute-start | bytes 884744 | tf_op jit(solution)/shard_map/ppermute | solution.py:441
  (146 other events, 1481.8 us)
